TPU v7x, 32 devices: a whole 2x2x4 slice. The times are simulated.
32 devices in a mesh: groups: 2 (over y), dom: 4 (over z), mp: 4 (over x, core).
Axes of the slice: x: 2, y: 2, z: 4, core: 2. Of those that a mesh axis runs over, the one named last changes fastest.
Arguments:
- nodes: float32 [1536, 512], P(('groups', 'dom', 'mp')), parts along dimension 0, may hold values from -6 to 6
- edges: float32 [12288, 512], P(('groups', 'dom', 'mp')), parts along dimension 0, may hold values from -6 to 6
- senders: int32 [6144], P(('dom', 'mp')), may hold values from 0 to 71
- receivers: int32 [6144], P(('dom', 'mp')), may hold values from 0 to 48, as said below
- halo_rows: int32 [384], P(('dom', 'mp')), may hold values from 0 to 47
- drop_mask: int32 [6144], P(('dom', 'mp')), may hold values 0 or 1
- w_in: float32 [1536, 512], P('mp'), may hold values from -0.15625 to 0.15625
- w_out: float32 [512, 512], P('mp'), may hold values from -0.25 to 0.25
- cotangent: float32 [12288, 512], P(('groups', 'dom', 'mp')), parts along dimension 0, may hold values from -6 to 6
Outputs:
- grad_nodes: float32 [1536, 512], P(('groups', 'dom', 'mp')), parts along dimension 0
- grad_edges: float32 [12288, 512], P(('groups', 'dom', 'mp')), parts along dimension 0
- grad_w_in: float32 [3072, 512], P(('groups', 'mp')), parts along dimension 0
- grad_w_out: float32 [1024, 512], P(('groups', 'mp')), parts along dimension 0
There are 2 independent parts, one for each index of `groups`. A program takes and returns all parts, laid end to end along the dimension named above; an argument that names none is the same for every part. Nothing has to cross between parts.
Inputs may be any that keep to these rules, and one draw needn't show every extreme that they name: `receivers`: each partition's 384 ids are non-decreasing and start at 0; ids below 48 name a node of that partition, 48 marks padding, and every partition has some padding at its end and real edges in at least half of its slots.
All inputs are finite; a program needn't handle non-finite values. No bound on the sum of `drop_mask` on one device may be relied on, other than what follows from the above.
Results may differ from a plain program's by a relative error of at most 0.00012.
Values sent between devices are 32-bit elements; how exact they have to be, the bound alone decides.
A program may use at most 64 MiB of HBM per device.

v0:
```python
import math

import jax
import jax.numpy as jnp
from jax import lax
from jax.sharding import PartitionSpec as P

norm_epsilon = 1e-05
keep_scale = 1.0 / 0.9


def passed_along(value, axis, steps):
    count = lax.axis_size(axis)
    pairs = [(source, (source + steps) % count) for source in range(count)]
    return lax.ppermute(value, axis, pairs)


def matmul(left, right):
    return jnp.dot(left, right, preferred_element_type=jnp.float32, precision=lax.Precision.HIGHEST)


def body(nodes, edges, senders, receivers, halo_rows, drop_mask, w_in, w_out, cotangent):
    count_nodes = nodes.shape[0]
    count_edges = edges.shape[0]
    halo_size = halo_rows.shape[0] // 2
    first_rows = halo_rows[:halo_size]
    last_rows = halo_rows[halo_size:]
    full_in, full_out = (
        lax.all_gather(w_in, "mp", axis=0, tiled=True),
        lax.all_gather(w_out, "mp", axis=0, tiled=True),
    )
    from_prev = passed_along(nodes[first_rows], ("dom", "mp"), 1)
    from_next = passed_along(nodes[last_rows], ("dom", "mp"), -1)
    table = jnp.concatenate([nodes, from_prev, from_next], axis=0)
    target_rows = jnp.minimum(receivers, count_nodes - 1)
    keep = jnp.where(
        (receivers < count_nodes) & (drop_mask == 1), jnp.float32(keep_scale), jnp.float32(0.0)
    )[:, None]

    def local_layer(table_in, edge_in, first, second):
        joined = jnp.concatenate([edge_in, table_in[senders], table_in[target_rows]], axis=1)
        hidden_in = matmul(joined, first)
        hidden = hidden_in * jax.nn.sigmoid(hidden_in)
        message = matmul(hidden, second)
        centre = jnp.mean(message, axis=1, keepdims=True)
        variance = jnp.mean(message * message, axis=1, keepdims=True) - centre * centre
        normed = (message - centre) * lax.rsqrt(variance + norm_epsilon)
        return edge_in + keep * normed

    updated, pullback = jax.vjp(local_layer, table, edges, full_in, full_out)
    grad_table, grad_edges, grad_first, grad_second = pullback(cotangent)
    back_prev = passed_along(grad_table[count_nodes : count_nodes + halo_size], ("dom", "mp"), -1)
    back_next = passed_along(grad_table[count_nodes + halo_size :], ("dom", "mp"), 1)
    grad_nodes = grad_table[:count_nodes].at[first_rows].add(back_prev).at[last_rows].add(back_next)
    share_in, share_out = (
        lax.psum_scatter(grad_first, "mp", scatter_dimension=0, tiled=True),
        lax.psum_scatter(grad_second, "mp", scatter_dimension=0, tiled=True),
    )
    summed_in, summed_out = lax.psum((share_in, share_out), "dom")
    factor = 1.0 / math.sqrt(count_edges * lax.axis_size("dom") * lax.axis_size("mp"))
    return (grad_nodes, grad_edges, summed_in * factor, summed_out * factor)


def solution(mesh):
    return jax.shard_map(
        body,
        mesh=mesh,
        in_specs=(
            P(("groups", "dom", "mp"), None),
            P(("groups", "dom", "mp"), None),
            P(("dom", "mp")),
            P(("dom", "mp")),
            P(("dom", "mp")),
            P(("dom", "mp")),
            P("mp", None),
            P("mp", None),
            P(("groups", "dom", "mp"), None),
        ),
        out_specs=(
            P(("groups", "dom", "mp"), None),
            P(("groups", "dom", "mp"), None),
            P(("groups", "mp"), None),
            P(("groups", "mp"), None),
        ),
        check_vma=False,
    )
```

profile of v0, /device:TPU:0, one launch (start us, length us, event | category | flops | bytes accessed | tf_op | source)
XLA Modules:
  0.0 197.0 jit_solution(10978852431515018588)
XLA Ops:
  7.3 0.7 all-gather.3.cloned.1.call-update
  8.0 0.8 compare_select_fusion.3
  8.8 1.5 gather_fusion.1
  10.3 5.5 %collective-permute-start.1 = (f32[12,512]{1,0:T(8,128)S(1)}, f32[12,512]{1,0:T(8,128)S(1)}, u32[]{:S(2)}, u32[]{:S(2)}) collective-permute-start(f32[12,512]{1,0:T(8,128)S(1)} %gather_fusion.1), channel_id=1, source_target_pairs={{0,15},{1,0},{2,1},{3,2},{4,3},{5,4},{6,5},{7,6},{8,7},{9,8},{10,9... | collective-permute-start | bytes 73736 | tf_op jit(solution)/shard_map/ppermute | solution.py:15
  15.7 1.5 gather_fusion
  17.4 1.2 constant_dynamic-update-slice_fusion.2
  18.7 4.7 %collective-permute-done = f32[12,512]{1,0:T(8,128)S(1)} collective-permute-done((f32[12,512]{1,0:T(8,128)S(1)}, f32[12,512]{1,0:T(8,128)S(1)}, u32[]{:S(2)}, u32[]{:S(2)}) %collective-permute-start) | collective-permute-done | bytes 24608 | tf_op jit(solution)/shard_map/ppermute | solution.py:15
  23.4 1.6 gather_fusion.2
  25.1 2.2 %gather_fusion.3 = f32[384,512]{1,0:T(8,128)} fusion(f32[72,512]{1,0:T(8,128)S(1)} %pad_maximum_fusion, s32[1024]{0:T(1024)S(1)} %get-tuple-element.19), kind=kCustom, calls=%fused_computation.3 | custom fusion | bytes 1574400 | tf_op jit(solution)/shard_map/jvp()/gather | solution.py:41
  27.4 1.2 constant_dynamic-update-slice_fusion
  28.6 12.7 %all-gather.3.cloned.1.call-done = f32[1536,512]{1,0:T(8,128)} async-done(((f32[384,512]{1,0:T(8,128)}), f32[1536,512]{1,0:T(8,128)}) %all-gather.3.cloned.1.call-update) | async-done | bytes 3145744 | tf_op jit(solution)/shard_map/all_gather | solution.py:29
  41.2 5.9 %fusion.26 = f32[384,512]{1,0:T(8,128)S(1)} fusion(f32[384,1536]{1,0:T(8,128)S(1)} %constant_dynamic-update-slice_fusion, f32[1536,512]{1,0:T(8,128)} %all-gather.3.cloned.1.call-done), kind=kOutput, calls=%fused_computation.55 | convolution fusion | flops 3623878656 | bytes 6291456 | tf_op jit(solution)/shard_map/jvp()/dot_general | solution.py:19
  47.1 12.1 %all-gather.5.cloned.1.call-done = f32[512,512]{1,0:T(8,128)} async-done(((f32[128,512]{1,0:T(8,128)}), f32[512,512]{1,0:T(8,128)}) %all-gather.5.cloned.1.call-update) | async-done | bytes 1048592 | tf_op jit(solution)/shard_map/all_gather | solution.py:30
  59.2 3.0 %multiply_reduce_fusion.1 = (f32[384]{0:T(512)S(1)}, f32[384]{0:T(512)S(1)}, f32[384,512]{1,0:T(8,128)S(1)}) fusion(f32[512,512]{1,0:T(8,128)} %all-gather.5.cloned.1.call-done, f32[384,512]{1,0:T(8,128)S(1)} %fusion.26), kind=kOutput, calls=%fused_computation.19 | convolution fusion | flops 1209335040 | bytes 2624512 | tf_op jit(solution)/shard_map/jvp()/dot_general | solution.py:19
  62.6 0.5 copy-done.7
  63.1 3.2 %fusion.8 = f32[512,512]{1,0:T(8,128)} fusion(f32[384,512]{1,0:T(8,128)S(1)} %fusion.26, f32[384,512]{1,0:T(8,128)S(1)} %get-tuple-element.18, f32[384,512]{1,0:T(8,128)S(1)} %copy-done.3, f32[384]{0:T(512)S(1)} %fusion.14, f32[384]{0:T(512)S(1)} %get-tuple-element.10, f32[384]{0:T(512)S(1)} %get-tuple-element.15, f32[384]{0:T(512)S(1)} %and_select_fusion), kind=kOutput, calls=%fused_computation.25 | convolution fusion | flops 1209925632 | bytes 3414016 | tf_op jit(solution)/shard_map/transpose(jvp())/dot_general | solution.py:19
  66.5 3.3 %fusion.23 = f32[384,512]{1,0:T(8,128)S(1)} fusion(f32[512,512]{1,0:T(8,128)} %all-gather.5.cloned.1.call-done, f32[384,512]{1,0:T(8,128)} %copy-done.7, f32[384,512]{1,0:T(8,128)} %param.17, f32[384]{0:T(512)S(1)} %fusion.14, f32[384]{0:T(512)S(1)} %get-tuple-element.10, f32[384]{0:T(512)S(1)} %get-tuple-element.15, f32[384]{0:T(512)S(1)} %and_select_fusion), kind=kOutput, calls=%fused_computation.53 | convolution fusion | flops 1209139200 | bytes 3414016 | tf_op jit(solution)/shard_map/transpose(jvp())/dot_general | solution.py:19
  69.9 0.9 copy-done.2
  70.8 7.0 %fusion.18 = f32[1536,512]{1,0:T(8,128)} fusion(f32[384,1536]{1,0:T(8,128)S(1)} %constant_dynamic-update-slice_fusion, f32[384,512]{1,0:T(8,128)S(1)} %fusion.26, f32[384,512]{1,0:T(8,128)S(1)} %fusion.23), kind=kOutput, calls=%fused_computation.51 | convolution fusion | flops 3625648128 | bytes 7077888 | tf_op jit(solution)/shard_map/transpose(jvp())/dot_general | solution.py:19
  78.1 13.3 %reduce-scatter.5.cloned.1.call-done = f32[128,512]{1,0:T(8,128)} async-done(((f32[512,512]{1,0:T(8,128)}), f32[128,512]{1,0:T(8,128)}) %reduce-scatter.5.cloned.1.call-update) | async-done | bytes 262160 | tf_op jit(solution)/shard_map/reduce_scatter | solution.py:57
  91.4 40.5 %reduce-scatter.3.cloned.1.call-done = f32[384,512]{1,0:T(8,128)} async-done(((f32[1536,512]{1,0:T(8,128)}), f32[384,512]{1,0:T(8,128)}) %reduce-scatter.3.cloned.1.call-update) | async-done | bytes 786448 | tf_op jit(solution)/shard_map/reduce_scatter | solution.py:56
  131.9 7.0 %fusion.20 = f32[384,1536]{1,0:T(8,128)} fusion(f32[1536,512]{1,0:T(8,128)S(1)} %copy-done, f32[384,512]{1,0:T(8,128)} %copy-done.1, f32[384,512]{1,0:T(8,128)} %copy-done.2), kind=kOutput, calls=%fused_computation.52 | convolution fusion | flops 3625648128 | bytes 7077888 | tf_op jit(solution)/shard_map/transpose(jvp())/dot_general | solution.py:19
  138.9 3.9 %scatter_custom_fusion = f32[72,512]{1,0:T(8,128)S(1)} fusion(s32[384]{0:T(512)S(1)} %compare_select_fusion.1, f32[384,1536]{1,0:T(8,128)} %fusion.20, f32[]{:T(128)} %constant.12.clone.1), kind=kCustom, calls=%fused_computation.16 | custom fusion | flops 196608 | bytes 934400 | tf_op jit(solution)/shard_map/transpose(jvp())/scatter-add | solution.py:41
  142.8 3.5 %scatter_custom_fusion.1 = f32[72,512]{1,0:T(8,128)S(1)} fusion(s32[384]{0:T(512)S(1)} %compare_select_fusion, f32[384,1536]{1,0:T(8,128)} %fusion.20, f32[]{:T(128)} %constant.12.clone.1), kind=kCustom, calls=%fused_computation.14 | custom fusion | flops 196608 | bytes 934400 | tf_op jit(solution)/shard_map/transpose(jvp())/scatter-add | solution.py:41
  146.3 2.8 %collective-permute-start.2 = (f32[12,512]{1,0:T(8,128)S(1)}, f32[12,512]{1,0:T(8,128)S(1)}, u32[]{:S(2)}, u32[]{:S(2)}) collective-permute-start(f32[12,512]{1,0:T(8,128)S(1)} %get-tuple-element.13), channel_id=1, source_target_pairs={{0,15},{1,0},{2,1},{3,2},{4,3},{5,4},{6,5},{7,6},{8,7},{9,8},{10,9... | collective-permute-start | bytes 73736 | tf_op jit(solution)/shard_map/ppermute | solution.py:15
  149.1 2.2 %slice_add_fusion = f32[384,512]{1,0:T(8,128)} fusion(f32[384,512]{1,0:T(8,128)S(1)} %copy-done.4, f32[384,1536]{1,0:T(8,128)} %fusion.20), kind=kLoop, calls=%fused_computation.13 | loop fusion | flops 196608 | bytes 2359296 | tf_op jit(solution)/shard_map/transpose(jvp())/add_any | solution.py:41
  151.4 0.7 scatter_fusion
  152.1 3.9 %collective-permute-done.3 = f32[12,512]{1,0:T(8,128)S(1)} collective-permute-done((f32[12,512]{1,0:T(8,128)S(1)}, f32[12,512]{1,0:T(8,128)S(1)}, u32[]{:S(2)}, u32[]{:S(2)}) %collective-permute-start.3) | collective-permute-done | bytes 24608 | tf_op jit(solution)/shard_map/ppermute | solution.py:15
  156.0 0.7 scatter_fusion.1
  156.7 30.0 %all-reduce.3.cloned.1.call-done = (f32[384,512]{1,0:T(8,128)}, f32[128,512]{1,0:T(8,128)}) async-done(((f32[384,512]{1,0:T(8,128)}, f32[128,512]{1,0:T(8,128)}), (f32[384,512]{1,0:T(8,128)}, f32[128,512]{1,0:T(8,128)})) %all-reduce.3.cloned.1.call-update) | async-done | bytes 1048592 | tf_op jit(solution)/shard_map/psum | solution.py:59
  186.7 2.1 %broadcast_multiply_fusion = f32[384,512]{1,0:T(8,128)} fusion(f32[384,512]{1,0:T(8,128)} %get-tuple-element.8), kind=kLoop, calls=%fused_computation.23 | loop fusion | flops 196608 | bytes 1572864 | tf_op jit(solution)/shard_map/mul | solution.py:61
  188.8 1.7 broadcast_multiply_fusion.1
  (48 shorter events, 1.4 us)
Async XLA Ops:
  7.2 16.3 %copy-start.6 = (f32[48,512]{1,0:T(8,128)S(1)}, f32[48,512]{1,0:T(8,128)}, u32[]{:S(2)}) copy-start(f32[48,512]{1,0:T(8,128)} %param.9) | copy-start | bytes 294916
  7.2 11.4 %copy-start.8 = (s32[384]{0:T(512)S(1)}, s32[384]{0:T(512)}, u32[]{:S(2)}) copy-start(s32[384]{0:T(512)} %param.12) | copy-start | bytes 4612
  7.2 11.4 %copy-start.10 = (s32[384]{0:T(512)S(1)}, s32[384]{0:T(512)}, u32[]{:S(2)}) copy-start(s32[384]{0:T(512)} %param.11) | copy-start | bytes 4612
  7.2 11.5 %copy-start.9 = (s32[384]{0:T(512)S(1)}, s32[384]{0:T(512)}, u32[]{:S(2)}) copy-start(s32[384]{0:T(512)} %param.14) | copy-start | bytes 4612
  7.2 34.0 %all-gather.3.cloned.1.call-start = ((), (), s32[]{:S(2)}) async-start(), calls=%async_computation.2 | async-start | bytes 3932160 | tf_op jit(solution)/shard_map/all_gather | solution.py:29
  7.9 51.2 %all-gather.5.cloned.1.call-start = ((), (), s32[]{:S(2)}) async-start(), calls=%async_computation.3 | async-start | bytes 1310720 | tf_op jit(solution)/shard_map/all_gather | solution.py:30
  10.3 8.4 %collective-permute-start.1 = (f32[12,512]{1,0:T(8,128)S(1)}, f32[12,512]{1,0:T(8,128)S(1)}, u32[]{:S(2)}, u32[]{:S(2)}) collective-permute-start(f32[12,512]{1,0:T(8,128)S(1)} %gather_fusion.1), channel_id=1, source_target_pairs={{0,15},{1,0},{2,1},{3,2},{4,3},{5,4},{6,5},{7,6},{8,7},{9,8},{10,9... | collective-permute-start | bytes 73736 | tf_op jit(solution)/shard_map/ppermute | solution.py:15
  17.2 6.2 %collective-permute-start = (f32[12,512]{1,0:T(8,128)S(1)}, f32[12,512]{1,0:T(8,128)S(1)}, u32[]{:S(2)}, u32[]{:S(2)}) collective-permute-start(f32[12,512]{1,0:T(8,128)S(1)} %gather_fusion), channel_id=1, source_target_pairs={{0,1},{1,2},{2,3},{3,4},{4,5},{5,6},{6,7},{7,8},{8,9},{9,10},{10,1... | collective-permute-start | bytes 73736 | tf_op jit(solution)/shard_map/ppermute | solution.py:15
  17.3 74.1 %reduce-scatter.5.cloned.1.call-start = ((), (), s32[]{:S(2)}) async-start(), calls=%async_computation.5 | async-start | bytes 1310720 | tf_op jit(solution)/shard_map/reduce_scatter | solution.py:57
  47.1 22.8 %copy-start.1 = (f32[384,512]{1,0:T(8,128)}, f32[384,512]{1,0:T(8,128)S(1)}, u32[]{:S(2)}) copy-start(f32[384,512]{1,0:T(8,128)S(1)} %fusion.26) | copy-start | bytes 2359300
  59.2 3.0 %copy-start.3 = (f32[384,512]{1,0:T(8,128)S(1)}, f32[384,512]{1,0:T(8,128)}, u32[]{:S(2)}) copy-start(f32[384,512]{1,0:T(8,128)} %param.17) | copy-start | bytes 2359300
  62.2 0.9 copy-start.7
  66.3 65.6 %reduce-scatter.3.cloned.1.call-start = ((), (), s32[]{:S(2)}) async-start(), calls=%async_computation.4 | async-start | bytes 3932160 | tf_op jit(solution)/shard_map/reduce_scatter | solution.py:56
  69.9 0.9 copy-start.2
  77.8 54.2 %copy-start = (f32[1536,512]{1,0:T(8,128)S(1)}, f32[1536,512]{1,0:T(8,128)}, u32[]{:S(2)}) copy-start(f32[1536,512]{1,0:T(8,128)} %all-gather.3.cloned.1.call-done) | copy-start | bytes 9437188
  77.8 109.0 %all-reduce.3.cloned.1.call-start = ((), (), s32[]{:S(2)}) async-start(), calls=%async_computation.6 | async-start | bytes 2097152 | tf_op jit(solution)/shard_map/psum | solution.py:59
  138.9 10.2 %copy-start.4 = (f32[384,512]{1,0:T(8,128)S(1)}, f32[384,512]{1,0:T(8,128)}, u32[]{:S(2)}) copy-start(f32[384,512]{1,0:T(8,128)} %param.17) | copy-start | bytes 2359300
  146.3 5.0 %collective-permute-start.2 = (f32[12,512]{1,0:T(8,128)S(1)}, f32[12,512]{1,0:T(8,128)S(1)}, u32[]{:S(2)}, u32[]{:S(2)}) collective-permute-start(f32[12,512]{1,0:T(8,128)S(1)} %get-tuple-element.13), channel_id=1, source_target_pairs={{0,15},{1,0},{2,1},{3,2},{4,3},{5,4},{6,5},{7,6},{8,7},{9,8},{10,9... | collective-permute-start | bytes 73736 | tf_op jit(solution)/shard_map/ppermute | solution.py:15
  149.1 6.9 %collective-permute-start.3 = (f32[12,512]{1,0:T(8,128)S(1)}, f32[12,512]{1,0:T(8,128)S(1)}, u32[]{:S(2)}, u32[]{:S(2)}) collective-permute-start(f32[12,512]{1,0:T(8,128)S(1)} %get-tuple-element.12), channel_id=1, source_target_pairs={{0,1},{1,2},{2,3},{3,4},{4,5},{5,6},{6,7},{7,8},{8,9},{9,10},{10,1... | collective-permute-start | bytes 73736 | tf_op jit(solution)/shard_map/ppermute | solution.py:15
  156.7 33.8 %copy-start.5 = (f32[48,512]{1,0:T(8,128)}, f32[48,512]{1,0:T(8,128)S(1)}, u32[]{:S(2)}) copy-start(f32[48,512]{1,0:T(8,128)S(1)} %scatter_fusion.1) | copy-start | bytes 294916
Sparse Core Ops, SparseCore 0:
  9.6 31.5 all-gather.2
  42.8 16.3 all-gather.4
  66.4 24.8 reduce-scatter.4
  93.9 37.9 reduce-scatter.2
  134.2 52.5 all-reduce.2
where the time goes:
time: 198 us; the launch traced here: 197 us
  waiting for transfers between devices  118 us (60%)
  matrix products  29.4 us (15%)
  other arithmetic  16 us (8%)
  between operations  14 us (7%)
  local copies, waits for them, and re-layouts  10.7 us (5%)
  starting transfers between devices  8.88 us (4%)
    reduce_scatter x1, waiting for transfers between devices, body(): lax.psum_scatter(grad_first, 'mp', scatter_dimension=0, tiled=True)  40.5 us
    psum x1, waiting for transfers between devices, body(): summed_in, summed_out = lax.psum((share_in, share_out), 'dom')  30 us
    dot_general x6, matrix products, matmul(): jnp.dot(left, right, preferred_element_type=jnp.float32, precision=lax.Pr...  29.4 us
    reduce_scatter x1, waiting for transfers between devices, body(): lax.psum_scatter(grad_second, 'mp', scatter_dimension=0, tiled=True)  13.3 us
    all_gather x1, waiting for transfers between devices, body(): lax.all_gather(w_in, 'mp', axis=0, tiled=True)  12.7 us
    all_gather x1, waiting for transfers between devices, body(): lax.all_gather(w_out, 'mp', axis=0, tiled=True)  12.1 us
    ppermute x4, waiting for transfers between devices, passed_along(): return lax.ppermute(value, axis, pairs)  8.73 us
    ppermute x4, starting transfers between devices, passed_along(): return lax.ppermute(value, axis, pairs)  8.28 us
  transfers between devices with their start and end apart: 9, of which 8 were waited for; matrix products, arithmetic and copies ran while one was open for 22% of the time, Pallas kernels for 0%

commit v1 on v0

v1 whole, which is shorter than its diff:
```python
import functools
import math

import jax
import jax.numpy as jnp
from jax import lax
from jax.experimental import pallas as pl
from jax.experimental.pallas import tpu as pltpu
from jax.sharding import PartitionSpec as P

norm_epsilon = 1e-05
keep_scale = 1.0 / 0.9
MESH = pl.DeviceIdType.MESH
f32, bf16 = jnp.float32, jnp.bfloat16


def split(value):
    high = value.astype(bf16)
    return high, (value - high.astype(f32)).astype(bf16)


def product(left, right, contract):
    return lax.dot_general(left, right, ((contract[:1], contract[1:]), ((), ())), preferred_element_type=f32)


def product3(left, right, contract):
    (lh, ll), (rh, rl) = left, right
    return product(lh, rh, contract) + (product(lh, rl, contract) + product(ll, rh, contract))


def product2(exact, right, contract):
    rh, rl = right
    return product(exact, rh, contract) + product(exact, rl, contract)


def pick(pair, rows):
    return pair[0][rows], pair[1][rows]


def kernel(
    sizes,
    nodes_ref, edges_ref, senders_ref, receivers_ref, halo_ref, drop_ref, win_ref, wout_ref, cot_ref,
    gnodes_ref, gedges_ref, gwin_ref, gwout_ref,
    table, full_in, full_out, halo_send, back_send, back_recv, gin, gout,
    from_core, x_send, from_x, acc, from_outer, from_inner, total,
    gather_send, gather_recv, halo_ssem, halo_rsem, core_ssem, core_rsem, x_ssem, x_rsem,
    outer_rsem, inner_rsem, inward_ssem, outward_ssem,
):
    groups, doms, chunk = sizes["groups"], sizes["dom"], sizes["chunk"]
    count_parts = doms * 4
    g, d, m = lax.axis_index("groups"), lax.axis_index("dom"), lax.axis_index("mp")
    x, c = m // 2, m % 2
    far = 1 - x
    part = d * 4 + m
    after, before = (part + 1) % count_parts, (part + count_parts - 1) % count_parts
    core_peer = (g, d, 2 * x + (1 - c))
    x_peer = (g, d, 2 * far + c)
    y_peer = (1 - g, d, m)
    next_peer = (g, after // 4, after % 4)
    prev_peer = (g, before // 4, before % 4)
    left_half = d < doms // 2
    inner = jnp.where(left_half, d + 1, d - 1)
    outer = jnp.where(left_half, d - 1, d + 1)
    has_outer = (d > 0) & (d < doms - 1)
    is_mid = (d == doms // 2 - 1) | (d == doms // 2)
    inner_peer, outer_peer = (g, inner, m), (g, outer, m)
    helped = groups == 2

    barrier = pltpu.get_barrier_semaphore()
    partners = [core_peer, x_peer, next_peer, prev_peer, inner_peer] + ([y_peer] if helped else [])
    for peer in partners:
        pl.semaphore_signal(barrier, inc=1, device_id=peer, device_id_type=MESH)

    @pl.when(has_outer)
    def _():
        pl.semaphore_signal(barrier, inc=1, device_id=outer_peer, device_id_type=MESH)
        pl.semaphore_wait(barrier, len(partners) + 1)

    @pl.when(jnp.logical_not(has_outer))
    def _():
        pl.semaphore_wait(barrier, len(partners))

    def remote(src, dst, send, recv, peer):
        return pltpu.make_async_remote_copy(
            src_ref=src, dst_ref=dst, send_sem=send, recv_sem=recv, device_id=peer, device_id_type=MESH
        )

    rows_in, rows_out = win_ref.shape[0], wout_ref.shape[0]
    depth = full_out.shape[0]
    count_nodes, count_edges = nodes_ref.shape[0], edges_ref.shape[0]
    padded = halo_send.shape[1]
    parts = 2 if helped else 1
    mine, other = (g, 1 - g) if helped else (0, 0)
    half_in, half_out = rows_in // parts, rows_out // parts
    pieces = [(0, 0, half_in // 2), (0, half_in // 2, half_in // 2), (1, 0, half_out)]

    def rows_at(start, size):
        return pl.ds(pl.multiple_of(start, 8), size)

    def piece_of(owner, which, number):
        kind, offset, size = pieces[number]
        if kind == 0:
            return full_in.at[rows_at(owner * rows_in + which * half_in + offset, size)]
        return full_out.at[rows_at(owner * rows_out + which * half_out + offset, size)]

    def own_piece(which, number):
        kind, offset, size = pieces[number]
        if kind == 0:
            return win_ref.at[rows_at(which * half_in + offset, size)]
        return wout_ref.at[rows_at(which * half_out + offset, size)]

    x_copies, y_copies, fx_copies, fy_copies = [], [], [], []
    for number in range(3):
        copy = remote(own_piece(mine, number), piece_of(m, mine, number), gather_send.at[1, number], gather_recv.at[1, number], x_peer)
        copy.start()
        x_copies.append(copy)
    whole_in = remote(win_ref, full_in.at[rows_at(m * rows_in, rows_in)], gather_send.at[0, 0], gather_recv.at[0, 0], core_peer)
    whole_out = remote(wout_ref, full_out.at[rows_at(m * rows_out, rows_out)], gather_send.at[0, 1], gather_recv.at[0, 1], core_peer)
    whole_in.start()
    whole_out.start()

    halo_hit = lax.broadcasted_iota(jnp.int32, (count_nodes, 128), 0) == halo_ref[...]
    halo_hot = jnp.where(halo_hit, 1.0, 0.0)
    halo_pick = jnp.transpose(halo_hot)[: 2 * padded].astype(bf16)
    halo_hot = halo_hot.astype(bf16)[:, : 2 * padded]
    nodes = nodes_ref[...]
    nh, nl = split(nodes)
    nr = (nodes - nh.astype(f32) - nl.astype(f32)).astype(bf16)
    listed = product(halo_pick, nh, (1, 0)) + (product(halo_pick, nl, (1, 0)) + product(halo_pick, nr, (1, 0)))
    halo_send[0] = listed[:padded]
    halo_send[1] = listed[padded:]
    first_at, last_at = pl.ds(count_nodes, padded), pl.ds(count_nodes + padded, padded)
    to_next = remote(halo_send.at[0], table.at[first_at], halo_ssem.at[0], halo_rsem.at[0], next_peer)
    to_prev = remote(halo_send.at[1], table.at[last_at], halo_ssem.at[1], halo_rsem.at[1], prev_peer)
    to_next.start()
    to_prev.start()
    slots = count_nodes + 2 * padded
    table[0:count_nodes] = nodes
    table[slots : slots + count_nodes] = nodes

    halo_size = sizes["halo"]
    senders = senders_ref[...]
    senders = jnp.where(senders < count_nodes + halo_size, senders, senders + (padded - halo_size))
    receivers = receivers_ref[...]
    targets = slots + jnp.minimum(receivers, count_nodes - 1)
    total_slots = slots + count_nodes
    index = lax.broadcasted_iota(jnp.int32, (total_slots, count_edges), 0)
    hot = jnp.where((index == senders) | (index == targets), 1.0, 0.0)
    hot_t = hot.astype(bf16)
    hot = jnp.transpose(hot).astype(bf16)
    keep = jnp.where((receivers < count_nodes) & (drop_ref[...] == 1), f32(keep_scale), f32(0.0))
    keep = jnp.transpose(jnp.broadcast_to(keep, (128, count_edges)))[:, :1]

    full_in[rows_at(m * rows_in, rows_in)] = win_ref[...]
    full_out[rows_at(m * rows_out, rows_out)] = wout_ref[...]
    edges = split(edges_ref[...])

    peer_x, peer_core, peer_far = 2 * far + c, 2 * x + (1 - c), 2 * far + (1 - c)

    def forward_x(number):
        x_copies[number].wait_recv()
        block = piece_of(peer_x, mine, number)
        copy = remote(block, block, gather_send.at[3, number], gather_recv.at[3, number], core_peer)
        if helped:
            along = remote(block, block, gather_send.at[2, number], gather_recv.at[2, number], y_peer)
            along.start()
            y_copies.append(along)
        copy.start()
        fx_copies.append(copy)

    def forward_y(number):
        if helped:
            y_copies[number].wait_recv()
            block = piece_of(peer_x, other, number)
            copy = remote(block, block, gather_send.at[4, number], gather_recv.at[4, number], core_peer)
            copy.start()
            fy_copies.append(copy)

    forward_x(0)
    forward_x(1)
    forward_y(0)
    forward_x(2)
    forward_y(1)
    whole_in.wait_recv()
    to_next.wait_recv()
    to_prev.wait_recv()
    for number in range(2):
        fx_copies[number].wait_recv()
        if helped:
            fy_copies[number].wait_recv()

    w_a = split(full_in[0:depth])
    w_b = split(full_in[depth : 2 * depth])
    w_c = split(full_in[2 * depth : 3 * depth])
    table_pair = split(table[...])
    ends = jnp.concatenate(
        [
            product3(pick(table_pair, slice(0, slots)), w_b, (1, 0)),
            product3(pick(table_pair, slice(slots, total_slots)), w_c, (1, 0)),
        ],
        axis=0,
    )
    hidden_in = product3(edges, w_a, (1, 0)) + product2(hot, split(ends), (1, 0))
    gate = jax.nn.sigmoid(hidden_in)
    hidden = split(hidden_in * gate)
    slope = gate + hidden_in * gate * (1.0 - gate)

    forward_y(2)
    whole_out.wait_recv()
    fx_copies[2].wait_recv()
    if helped:
        fy_copies[2].wait_recv()
    w_o = split(full_out[...])
    message = product3(hidden, w_o, (1, 0))
    centre = jnp.mean(message, axis=1, keepdims=True)
    variance = jnp.mean(message * message, axis=1, keepdims=True) - centre * centre
    scale = lax.rsqrt(variance + norm_epsilon)
    normed = (message - centre) * scale
    weighted = keep * cot_ref[...]
    grad_message = split(
        scale
        * (
            weighted
            - jnp.mean(weighted, axis=1, keepdims=True)
            - normed * jnp.mean(weighted * normed, axis=1, keepdims=True)
        )
    )
    gout[...] = product3(hidden, grad_message, (0, 0))

    blocks = [(1, start) for start in range(0, rows_out, chunk)] + [(0, start) for start in range(0, rows_in, chunk)]
    first_in = rows_out // chunk

    def grad_rows(owner, number):
        kind, start = blocks[number]
        if kind == 1:
            return gout.at[rows_at(owner * rows_out + start, chunk)]
        return gin.at[rows_at(owner * rows_in + start, chunk)]

    core_copies, x_grad_copies = {}, {}

    def swap_cores(numbers):
        for side, owner in ((0, peer_far), (1, peer_core)):
            for number in numbers:
                copy = remote(
                    grad_rows(owner, number), from_core.at[side, number],
                    core_ssem.at[side, number], core_rsem.at[side, number], core_peer,
                )
                copy.start()
                core_copies[side, number] = copy

    def swap_x(numbers):
        for number in numbers:
            core_copies[0, number].wait_recv()
            x_send[number] = grad_rows(peer_x, number)[...] + from_core[0, number]
            copy = remote(x_send.at[number], from_x.at[number], x_ssem.at[number], x_rsem.at[number], x_peer)
            copy.start()
            x_grad_copies[number] = copy

    early, late = range(first_in), range(first_in, len(blocks))
    swap_cores(early)
    grad_hidden = split(product3(grad_message, w_o, (1, 1)) * slope)
    swap_x(early)
    sums = product2(hot_t, grad_hidden, (1, 0))
    slot = lax.broadcasted_iota(jnp.int32, sums.shape, 0)
    gin[depth : 2 * depth] = product3(table_pair, split(jnp.where(slot < slots, sums, 0.0)), (0, 0))
    gin[2 * depth : 3 * depth] = product3(table_pair, split(jnp.where(slot < slots, 0.0, sums)), (0, 0))
    gin[0:depth] = product3(edges, grad_hidden, (0, 0))
    swap_cores(late)

    sums = split(sums)
    grad_table = product3(pick(sums, slice(0, slots)), w_b, (1, 1))
    back_send[0] = grad_table[count_nodes : count_nodes + padded]
    back_send[1] = grad_table[count_nodes + padded : slots]
    back_prev = remote(back_send.at[0], back_recv.at[pl.ds(0, padded)], halo_ssem.at[2], halo_rsem.at[2], prev_peer)
    back_next = remote(back_send.at[1], back_recv.at[pl.ds(padded, padded)], halo_ssem.at[3], halo_rsem.at[3], next_peer)
    back_prev.start()
    back_next.start()
    swap_x(late)
    own = grad_table[:count_nodes] + product3(pick(sums, slice(slots, total_slots)), w_c, (1, 1))
    gedges_ref[...] = cot_ref[...] + product3(grad_hidden, w_a, (1, 1))
    back_prev.wait_recv()
    back_next.wait_recv()
    gnodes_ref[...] = own + product2(halo_hot, split(back_recv[...]), (1, 0))

    def inward(number, to_mid):
        landing = (from_inner, inner_rsem) if to_mid else (from_outer, outer_rsem)
        return remote(acc.at[number], landing[0].at[number], inward_ssem.at[number], landing[1].at[number], inner_peer)

    def outward(number):
        return remote(total.at[number], from_inner.at[number], outward_ssem.at[number], inner_rsem.at[number], outer_peer)

    def collect(number):
        core_copies[1, number].wait_recv()
        x_grad_copies[number].wait_recv()
        acc[number] = grad_rows(m, number)[...] + from_core[1, number] + from_x[number]

        @pl.when(has_outer)
        def _():
            inward(number, False).wait_recv()
            acc[number] = acc[number] + from_outer[number]

        @pl.when(is_mid)
        def _():
            inward(number, True).start()

        @pl.when(jnp.logical_not(is_mid))
        def _():
            inward(number, False).start()

    factor = f32(sizes["factor"])

    def finish(number, sends):
        kind, start = blocks[number]
        inward(number, True).wait_recv()

        @pl.when(is_mid)
        def _():
            total[number] = acc[number] + from_inner[number]

        @pl.when(jnp.logical_not(is_mid))
        def _():
            total[number] = from_inner[number]

        if sends:
            outward(number).start()
        result = gwout_ref if kind == 1 else gwin_ref
        result[pl.ds(start, chunk)] = total[number] * factor

    lag = 2
    for number in range(len(blocks) + lag):
        if number < len(blocks):
            collect(number)
        if number >= lag:

            @pl.when(has_outer)
            def _():
                finish(number - lag, True)

    @pl.when(jnp.logical_not(has_outer))
    def _():
        for number in range(len(blocks)):
            finish(number, False)

    for copy in [whole_in, whole_out, to_next, to_prev, back_prev, back_next] + x_copies + y_copies + fx_copies + fy_copies:
        copy.wait_send()
    for number in range(len(blocks)):
        core_copies[0, number].wait_send()
        core_copies[1, number].wait_send()
        x_grad_copies[number].wait_send()
        inward(number, True).wait_send()

    @pl.when(has_outer)
    def _():
        for number in range(len(blocks)):
            outward(number).wait_send()


def body(mesh_shape, nodes, edges, senders, receivers, halo_rows, drop_mask, w_in, w_out, cotangent):
    count_nodes, depth = nodes.shape
    count_edges = edges.shape[0]
    halo_size = halo_rows.shape[0] // 2
    padded = -(-halo_size // 16) * 16
    doms = mesh_shape["dom"]
    chunk = math.gcd(w_in.shape[0], w_out.shape[0]) // 2
    count = (w_in.shape[0] + w_out.shape[0]) // chunk
    sizes = {
        "groups": mesh_shape["groups"],
        "dom": doms,
        "chunk": chunk,
        "halo": halo_size,
        "factor": 1.0 / math.sqrt(count_edges * doms * mesh_shape["mp"]),
    }
    gap = jnp.full((padded - halo_size,), -1, jnp.int32)
    rest = jnp.full((128 - 2 * padded,), -1, jnp.int32)
    halo = jnp.concatenate([halo_rows[:halo_size], gap, halo_rows[halo_size:], gap, rest])[None, :]
    vmem = pl.BlockSpec(memory_space=pltpu.VMEM)
    piece = (count, chunk, depth)
    dma = pltpu.SemaphoreType.DMA
    return pl.pallas_call(
        functools.partial(kernel, sizes),
        out_shape=(
            jax.ShapeDtypeStruct(nodes.shape, f32),
            jax.ShapeDtypeStruct(edges.shape, f32),
            jax.ShapeDtypeStruct(w_in.shape, f32),
            jax.ShapeDtypeStruct(w_out.shape, f32),
        ),
        in_specs=[vmem] * 9,
        out_specs=(vmem,) * 4,
        scratch_shapes=[
            pltpu.VMEM((2 * count_nodes + 2 * padded, depth), f32),
            pltpu.VMEM((3 * depth, depth), f32),
            pltpu.VMEM((depth, depth), f32),
            pltpu.VMEM((2, padded, depth), f32),
            pltpu.VMEM((2, padded, depth), f32),
            pltpu.VMEM((2 * padded, depth), f32),
            pltpu.VMEM((3 * depth, depth), f32),
            pltpu.VMEM((depth, depth), f32),
            pltpu.VMEM((2,) + piece, f32),
            pltpu.VMEM(piece, f32),
            pltpu.VMEM(piece, f32),
            pltpu.VMEM(piece, f32),
            pltpu.VMEM(piece, f32),
            pltpu.VMEM(piece, f32),
            pltpu.VMEM(piece, f32),
            dma((5, 3)),
            dma((5, 3)),
            dma((4,)),
            dma((4,)),
            dma((2, count)),
            dma((2, count)),
            dma((count,)),
            dma((count,)),
            dma((count,)),
            dma((count,)),
            dma((count,)),
            dma((count,)),
        ],
        compiler_params=pltpu.CompilerParams(
            collective_id=0, has_side_effects=True, vmem_limit_bytes=56 * 1024 * 1024
        ),
    )(
        nodes, edges, senders[None, :], receivers[None, :], halo, drop_mask[None, :], w_in, w_out, cotangent
    )


def solution(mesh):
    return jax.shard_map(
        functools.partial(body, dict(mesh.shape)),
        mesh=mesh,
        in_specs=(
            P(("groups", "dom", "mp"), None),
            P(("groups", "dom", "mp"), None),
            P(("dom", "mp")),
            P(("dom", "mp")),
            P(("dom", "mp")),
            P(("dom", "mp")),
            P("mp", None),
            P("mp", None),
            P(("groups", "dom", "mp"), None),
        ),
        out_specs=(
            P(("groups", "dom", "mp"), None),
            P(("groups", "dom", "mp"), None),
            P(("groups", "mp"), None),
            P(("groups", "mp"), None),
        ),
        check_vma=False,
    )
```

time: 198 us -> 86.3 us (0.44)
  waiting for transfers between devices: 118 us -> 0 us
  Pallas kernels: 0 us -> 76.4 us
  matrix products: 29.4 us -> 0 us
  other arithmetic: 16 us -> 0 us
  between operations: 14 us -> 0.65 us
  starting transfers between devices: 8.88 us -> 0 us
    pallas_call x0 -> x1, Pallas kernels: none -> 76.4 us  [body(): pl.pallas_call(functools.partial(kernel, sizes), out_shape=(jax.ShapeDtyp...]
    reduce_scatter x2 -> x0, waiting for transfers between devices: 53.8 us -> none  [the longest x1 40.5 us: body(): lax.psum_scatter(grad_first, 'mp', scatter_dimension=0, tiled=True)]
    psum x1 -> x0, waiting for transfers between devices: 30 us -> none  [body(): summed_in, summed_out = lax.psum((share_in, share_out), 'dom')]
    dot_general x6 -> x0, matrix products: 29.4 us -> none  [matmul(): jnp.dot(left, right, preferred_element_type=jnp.float32, precision=lax.Pr...]
    all_gather x2 -> x0, waiting for transfers between devices: 24.7 us -> none  [the longest x1 12.7 us: body(): lax.all_gather(w_in, 'mp', axis=0, tiled=True)]
    scatter-add x4 -> x0, other arithmetic: 8.81 us -> none  [the longest x1 3.87 us: local_layer(): table_in[target_rows]]
    ppermute x4 -> x0, waiting for transfers between devices: 8.73 us -> none  [passed_along(): return lax.ppermute(value, axis, pairs)]
    ppermute x4 -> x0, starting transfers between devices: 8.28 us -> none  [passed_along(): return lax.ppermute(value, axis, pairs)]
  transfers between devices with their start and end apart: 9 -> 0, of which waited for: 8 -> 0; matrix products, arithmetic and copies ran while one was open for 22% -> 0% of each run, Pallas kernels for 0% -> 0%
where the time goes in v1:
time: 86.3 us; the launch traced here: 85.9 us
  Pallas kernels  76.4 us (89%)
  local copies, waits for them, and re-layouts  8.89 us (10%)
    pallas_call x1, Pallas kernels, body(): pl.pallas_call(functools.partial(kernel, sizes), out_shape=(jax.ShapeDtyp...  76.4 us
    unnamed x14, local copies, waits for them, and re-layouts  5.8 us

profile of v1, /device:TPU:0, one launch (start us, length us, event | category | flops | bytes accessed | tf_op | source)
XLA Modules:
  0.0 85.9 jit_solution(2229267566510474458)
XLA Ops:
  0.6 0.8 fusion
  1.4 0.0 copy-start.2
  1.4 0.6 concatenate.3
  2.0 0.1 copy-done.2
  2.1 0.0 copy-start.3
  2.1 0.6 broadcast_in_dim.15.senders_ref
  2.7 0.1 copy-done.3
  2.8 0.0 copy-start.4
  2.8 0.6 broadcast_in_dim.16.receivers_ref
  3.4 0.1 copy-done.4
  3.5 0.6 broadcast_in_dim.19.drop_ref
  4.1 76.4 %shard_map.120 = (f32[48,512]{1,0:T(8,128)}, f32[384,512]{1,0:T(8,128)}, f32[384,512]{1,0:T(8,128)}, f32[128,512]{1,0:T(8,128)}) custom-call(f32[48,512]{1,0:T(8,128)} %nodes_ref.1, f32[384,512]{1,0:T(8,128)} %edges_ref.1, s32[1,384]{1,0:T(1,128)} %broadcast_in_dim.15.senders_ref, s32[1,384]{1,0:T(1,128)} %broadcast_in_dim.16.receivers_ref, ...), custom_call_target="tpu_custom_call" | custom-call | tf_op jit(solution)/shard_map/pallas_call | solution.py:379
  80.5 1.5 %copy.17 = f32[48,512]{1,0:T(8,128)} copy(f32[48,512]{1,0:T(8,128)} %get-tuple-element.10) | data formatting | bytes 196608
  82.0 0.0 copy-start
  82.0 2.1 %copy.18 = f32[384,512]{1,0:T(8,128)} copy(f32[384,512]{1,0:T(8,128)} %get-tuple-element.11) | data formatting | bytes 1572864
  84.1 0.0 copy-done
  84.1 0.0 copy-start.1
  84.1 0.9 %copy.19 = f32[384,512]{1,0:T(8,128)} copy(f32[384,512]{1,0:T(8,128)S(1)} %copy-done) | data formatting | bytes 1572864
  85.0 0.2 copy-done.1
  85.2 0.7 copy.20
  (2 shorter events, 0.0 us)
Async XLA Ops:
  1.4 0.7 copy-start.2
  2.1 0.7 copy-start.3
  2.8 0.7 copy-start.4
  82.0 2.1 %copy-start = (f32[384,512]{1,0:T(8,128)S(1)}, f32[384,512]{1,0:T(8,128)}, u32[]{:S(2)}) copy-start(f32[384,512]{1,0:T(8,128)} %get-tuple-element.12) | copy-start | bytes 2359300
  84.1 1.1 %copy-start.1 = (f32[128,512]{1,0:T(8,128)S(1)}, f32[128,512]{1,0:T(8,128)}, u32[]{:S(2)}) copy-start(f32[128,512]{1,0:T(8,128)} %get-tuple-element.13) | copy-start | bytes 786436

commit v2 on v1

--- a/solution.py
+++ b/solution.py
@@ -45,8 +45,9 @@
     from_core, x_send, from_x, acc, from_outer, from_inner, total,
     gather_send, gather_recv, halo_ssem, halo_rsem, core_ssem, core_rsem, x_ssem, x_rsem,
     outer_rsem, inner_rsem, inward_ssem, outward_ssem,
+    edges_in, cot, grad_edges, own, local_sem,
 ):
-    groups, doms, chunk = sizes["groups"], sizes["dom"], sizes["chunk"]
+    groups, doms = sizes["groups"], sizes["dom"]
     count_parts = doms * 4
     g, d, m = lax.axis_index("groups"), lax.axis_index("dom"), lax.axis_index("mp")
     x, c = m // 2, m % 2
@@ -66,6 +67,12 @@
     inner_peer, outer_peer = (g, inner, m), (g, outer, m)
     helped = groups == 2
 
+    loads = [
+        pltpu.make_async_copy(edges_ref, edges_in, local_sem.at[0]),
+        pltpu.make_async_copy(cot_ref, cot, local_sem.at[1]),
+        pltpu.make_async_copy(win_ref, full_in.at[pl.ds(pl.multiple_of(m * win_ref.shape[0], 8), win_ref.shape[0])], local_sem.at[2]),
+        pltpu.make_async_copy(wout_ref, full_out.at[pl.ds(pl.multiple_of(m * wout_ref.shape[0], 8), wout_ref.shape[0])], local_sem.at[3]),
+    ]
     barrier = pltpu.get_barrier_semaphore()
     partners = [core_peer, x_peer, next_peer, prev_peer, inner_peer] + ([y_peer] if helped else [])
     for peer in partners:
@@ -79,6 +86,9 @@
     @pl.when(jnp.logical_not(has_outer))
     def _():
         pl.semaphore_wait(barrier, len(partners))
+
+    for load in loads:
+        load.start()
 
     def remote(src, dst, send, recv, peer):
         return pltpu.make_async_remote_copy(
@@ -92,7 +102,15 @@
     parts = 2 if helped else 1
     mine, other = (g, 1 - g) if helped else (0, 0)
     half_in, half_out = rows_in // parts, rows_out // parts
-    pieces = [(0, 0, half_in // 2), (0, half_in // 2, half_in // 2), (1, 0, half_out)]
+    pieces, start = [], 0
+    for share in sizes["gather_in"]:
+        pieces.append((0, start, half_in * share // sum(sizes["gather_in"])))
+        start += pieces[-1][2]
+    count_in, start = len(pieces), 0
+    for share in sizes["gather_out"]:
+        pieces.append((1, start, half_out * share // sum(sizes["gather_out"])))
+        start += pieces[-1][2]
+    last = len(pieces)
 
     def rows_at(start, size):
         return pl.ds(pl.multiple_of(start, 8), size)
@@ -110,7 +128,7 @@
         return wout_ref.at[rows_at(which * half_out + offset, size)]
 
     x_copies, y_copies, fx_copies, fy_copies = [], [], [], []
-    for number in range(3):
+    for number in range(last):
         copy = remote(own_piece(mine, number), piece_of(m, mine, number), gather_send.at[1, number], gather_recv.at[1, number], x_peer)
         copy.start()
         x_copies.append(copy)
@@ -119,14 +137,18 @@
     whole_in.start()
     whole_out.start()
 
-    halo_hit = lax.broadcasted_iota(jnp.int32, (count_nodes, 128), 0) == halo_ref[...]
-    halo_hot = jnp.where(halo_hit, 1.0, 0.0)
-    halo_pick = jnp.transpose(halo_hot)[: 2 * padded].astype(bf16)
-    halo_hot = halo_hot.astype(bf16)[:, : 2 * padded]
+    halo_size = sizes["halo"]
+    halo_hit = lax.broadcasted_iota(jnp.int32, (count_nodes, 2 * halo_size), 0) == halo_ref[...].reshape(1, 2 * halo_size)
+    item = lax.broadcasted_iota(jnp.int32, (2 * halo_size, 2 * padded), 0)
+    place = item + jnp.where(item < halo_size, 0, padded - halo_size)
+    spread = lax.broadcasted_iota(jnp.int32, (2 * halo_size, 2 * padded), 1) == place
+    halo_hot = product(
+        jnp.where(halo_hit, 1.0, 0.0).astype(bf16), jnp.where(spread, 1.0, 0.0).astype(bf16), (1, 0)
+    ).astype(bf16)
     nodes = nodes_ref[...]
     nh, nl = split(nodes)
     nr = (nodes - nh.astype(f32) - nl.astype(f32)).astype(bf16)
-    listed = product(halo_pick, nh, (1, 0)) + (product(halo_pick, nl, (1, 0)) + product(halo_pick, nr, (1, 0)))
+    listed = product(halo_hot, nh, (0, 0)) + (product(halo_hot, nl, (0, 0)) + product(halo_hot, nr, (0, 0)))
     halo_send[0] = listed[:padded]
     halo_send[1] = listed[padded:]
     first_at, last_at = pl.ds(count_nodes, padded), pl.ds(count_nodes + padded, padded)
@@ -138,22 +160,21 @@
     table[0:count_nodes] = nodes
     table[slots : slots + count_nodes] = nodes
 
-    halo_size = sizes["halo"]
-    senders = senders_ref[...]
+    senders = senders_ref[...].reshape(1, count_edges)
     senders = jnp.where(senders < count_nodes + halo_size, senders, senders + (padded - halo_size))
-    receivers = receivers_ref[...]
+    receivers = receivers_ref[...].reshape(1, count_edges)
     targets = slots + jnp.minimum(receivers, count_nodes - 1)
     total_slots = slots + count_nodes
     index = lax.broadcasted_iota(jnp.int32, (total_slots, count_edges), 0)
     hot = jnp.where((index == senders) | (index == targets), 1.0, 0.0)
     hot_t = hot.astype(bf16)
     hot = jnp.transpose(hot).astype(bf16)
-    keep = jnp.where((receivers < count_nodes) & (drop_ref[...] == 1), f32(keep_scale), f32(0.0))
+    keep = jnp.where((receivers < count_nodes) & (drop_ref[...].reshape(1, count_edges) == 1), f32(keep_scale), f32(0.0))
     keep = jnp.transpose(jnp.broadcast_to(keep, (128, count_edges)))[:, :1]
 
-    full_in[rows_at(m * rows_in, rows_in)] = win_ref[...]
-    full_out[rows_at(m * rows_out, rows_out)] = wout_ref[...]
-    edges = split(edges_ref[...])
+    for load in loads:
+        load.wait()
+    edges = split(edges_in[...])
 
     peer_x, peer_core, peer_far = 2 * far + c, 2 * x + (1 - c), 2 * far + (1 - c)
 
@@ -176,15 +197,16 @@
             copy.start()
             fy_copies.append(copy)
 
-    forward_x(0)
-    forward_x(1)
-    forward_y(0)
-    forward_x(2)
-    forward_y(1)
+    ahead = 2
+    for number in range(count_in + ahead):
+        if number < last:
+            forward_x(number)
+        if number >= ahead:
+            forward_y(number - ahead)
     whole_in.wait_recv()
     to_next.wait_recv()
     to_prev.wait_recv()
-    for number in range(2):
+    for number in range(count_in):
         fx_copies[number].wait_recv()
         if helped:
             fy_copies[number].wait_recv()
@@ -205,18 +227,22 @@
     hidden = split(hidden_in * gate)
     slope = gate + hidden_in * gate * (1.0 - gate)
 
-    forward_y(2)
+    for number in range(count_in, last):
+        if number >= count_in + ahead:
+            forward_x(number)
+        forward_y(number)
     whole_out.wait_recv()
-    fx_copies[2].wait_recv()
-    if helped:
-        fy_copies[2].wait_recv()
+    for number in range(count_in, last):
+        fx_copies[number].wait_recv()
+        if helped:
+            fy_copies[number].wait_recv()
     w_o = split(full_out[...])
     message = product3(hidden, w_o, (1, 0))
     centre = jnp.mean(message, axis=1, keepdims=True)
     variance = jnp.mean(message * message, axis=1, keepdims=True) - centre * centre
     scale = lax.rsqrt(variance + norm_epsilon)
     normed = (message - centre) * scale
-    weighted = keep * cot_ref[...]
+    weighted = keep * cot[...]
     grad_message = split(
         scale
         * (
@@ -227,14 +253,22 @@
     )
     gout[...] = product3(hidden, grad_message, (0, 0))
 
-    blocks = [(1, start) for start in range(0, rows_out, chunk)] + [(0, start) for start in range(0, rows_in, chunk)]
-    first_in = rows_out // chunk
+    blocks, at, start = [], 0, 0
+    for share in sizes["sum_out"]:
+        size = rows_out * share // sum(sizes["sum_out"])
+        blocks.append((1, start, pl.ds(at, size)))
+        start, at = start + size, at + size
+    first_in, start = len(blocks), 0
+    for share in sizes["sum_in"]:
+        size = rows_in * share // sum(sizes["sum_in"])
+        blocks.append((0, start, pl.ds(at, size)))
+        start, at = start + size, at + size
 
     def grad_rows(owner, number):
-        kind, start = blocks[number]
+        kind, start, span = blocks[number]
         if kind == 1:
-            return gout.at[rows_at(owner * rows_out + start, chunk)]
-        return gin.at[rows_at(owner * rows_in + start, chunk)]
+            return gout.at[rows_at(owner * rows_out + start, span.size)]
+        return gin.at[rows_at(owner * rows_in + start, span.size)]
 
     core_copies, x_grad_copies = {}, {}
 
@@ -242,7 +276,7 @@
         for side, owner in ((0, peer_far), (1, peer_core)):
             for number in numbers:
                 copy = remote(
-                    grad_rows(owner, number), from_core.at[side, number],
+                    grad_rows(owner, number), from_core.at[side, blocks[number][2]],
                     core_ssem.at[side, number], core_rsem.at[side, number], core_peer,
                 )
                 copy.start()
@@ -251,8 +285,8 @@
     def swap_x(numbers):
         for number in numbers:
             core_copies[0, number].wait_recv()
-            x_send[number] = grad_rows(peer_x, number)[...] + from_core[0, number]
-            copy = remote(x_send.at[number], from_x.at[number], x_ssem.at[number], x_rsem.at[number], x_peer)
+            x_send[blocks[number][2]] = grad_rows(peer_x, number)[...] + from_core[0, blocks[number][2]]
+            copy = remote(x_send.at[blocks[number][2]], from_x.at[blocks[number][2]], x_ssem.at[number], x_rsem.at[number], x_peer)
             copy.start()
             x_grad_copies[number] = copy
 
@@ -276,28 +310,27 @@
     back_prev.start()
     back_next.start()
     swap_x(late)
-    own = grad_table[:count_nodes] + product3(pick(sums, slice(slots, total_slots)), w_c, (1, 1))
-    gedges_ref[...] = cot_ref[...] + product3(grad_hidden, w_a, (1, 1))
-    back_prev.wait_recv()
-    back_next.wait_recv()
-    gnodes_ref[...] = own + product2(halo_hot, split(back_recv[...]), (1, 0))
+    own[...] = grad_table[:count_nodes] + product3(pick(sums, slice(slots, total_slots)), w_c, (1, 1))
+    grad_edges[...] = cot[...] + product3(grad_hidden, w_a, (1, 1))
+    edges_out = pltpu.make_async_copy(grad_edges, gedges_ref, local_sem.at[4])
+    edges_out.start()
 
     def inward(number, to_mid):
         landing = (from_inner, inner_rsem) if to_mid else (from_outer, outer_rsem)
-        return remote(acc.at[number], landing[0].at[number], inward_ssem.at[number], landing[1].at[number], inner_peer)
+        return remote(acc.at[blocks[number][2]], landing[0].at[blocks[number][2]], inward_ssem.at[number], landing[1].at[number], inner_peer)
 
     def outward(number):
-        return remote(total.at[number], from_inner.at[number], outward_ssem.at[number], inner_rsem.at[number], outer_peer)
+        return remote(total.at[blocks[number][2]], from_inner.at[blocks[number][2]], outward_ssem.at[number], inner_rsem.at[number], outer_peer)
 
     def collect(number):
         core_copies[1, number].wait_recv()
         x_grad_copies[number].wait_recv()
-        acc[number] = grad_rows(m, number)[...] + from_core[1, number] + from_x[number]
+        acc[blocks[number][2]] = grad_rows(m, number)[...] + from_core[1, blocks[number][2]] + from_x[blocks[number][2]]
 
         @pl.when(has_outer)
         def _():
             inward(number, False).wait_recv()
-            acc[number] = acc[number] + from_outer[number]
+            acc[blocks[number][2]] = acc[blocks[number][2]] + from_outer[blocks[number][2]]
 
         @pl.when(is_mid)
         def _():
@@ -310,26 +343,30 @@
     factor = f32(sizes["factor"])
 
     def finish(number, sends):
-        kind, start = blocks[number]
+        kind, start, span = blocks[number]
         inward(number, True).wait_recv()
 
         @pl.when(is_mid)
         def _():
-            total[number] = acc[number] + from_inner[number]
+            total[blocks[number][2]] = acc[blocks[number][2]] + from_inner[blocks[number][2]]
 
         @pl.when(jnp.logical_not(is_mid))
         def _():
-            total[number] = from_inner[number]
+            total[blocks[number][2]] = from_inner[blocks[number][2]]
 
         if sends:
             outward(number).start()
         result = gwout_ref if kind == 1 else gwin_ref
-        result[pl.ds(start, chunk)] = total[number] * factor
+        result[pl.ds(start, span.size)] = total[blocks[number][2]] * factor
 
     lag = 2
     for number in range(len(blocks) + lag):
         if number < len(blocks):
             collect(number)
+        if number == 4:
+            back_prev.wait_recv()
+            back_next.wait_recv()
+            gnodes_ref[...] = own[...] + product2(halo_hot, split(back_recv[...]), (1, 0))
         if number >= lag:
 
             @pl.when(has_outer)
@@ -341,6 +378,7 @@
         for number in range(len(blocks)):
             finish(number, False)
 
+    edges_out.wait()
     for copy in [whole_in, whole_out, to_next, to_prev, back_prev, back_next] + x_copies + y_copies + fx_copies + fy_copies:
         copy.wait_send()
     for number in range(len(blocks)):
@@ -361,20 +399,21 @@
     halo_size = halo_rows.shape[0] // 2
     padded = -(-halo_size // 16) * 16
     doms = mesh_shape["dom"]
-    chunk = math.gcd(w_in.shape[0], w_out.shape[0]) // 2
-    count = (w_in.shape[0] + w_out.shape[0]) // chunk
     sizes = {
         "groups": mesh_shape["groups"],
         "dom": doms,
-        "chunk": chunk,
+        "gather_in": (3, 3, 3, 2, 1),
+        "gather_out": (1, 1),
+        "sum_out": (1, 1, 2, 4),
+        "sum_in": (8, 8, 8, 8, 4, 4, 2, 2, 2, 1, 1),
         "halo": halo_size,
         "factor": 1.0 / math.sqrt(count_edges * doms * mesh_shape["mp"]),
     }
-    gap = jnp.full((padded - halo_size,), -1, jnp.int32)
-    rest = jnp.full((128 - 2 * padded,), -1, jnp.int32)
-    halo = jnp.concatenate([halo_rows[:halo_size], gap, halo_rows[halo_size:], gap, rest])[None, :]
     vmem = pl.BlockSpec(memory_space=pltpu.VMEM)
-    piece = (count, chunk, depth)
+    pieces = len(sizes["gather_in"]) + len(sizes["gather_out"])
+    count = len(sizes["sum_in"]) + len(sizes["sum_out"])
+    piece = (w_in.shape[0] + w_out.shape[0], depth)
+    hbm = pl.BlockSpec(memory_space=pl.ANY)
     dma = pltpu.SemaphoreType.DMA
     return pl.pallas_call(
         functools.partial(kernel, sizes),
@@ -384,8 +423,8 @@
             jax.ShapeDtypeStruct(w_in.shape, f32),
             jax.ShapeDtypeStruct(w_out.shape, f32),
         ),
-        in_specs=[vmem] * 9,
-        out_specs=(vmem,) * 4,
+        in_specs=[vmem, hbm, vmem, vmem, vmem, vmem, hbm, hbm, hbm],
+        out_specs=(vmem, hbm, vmem, vmem),
         scratch_shapes=[
             pltpu.VMEM((2 * count_nodes + 2 * padded, depth), f32),
             pltpu.VMEM((3 * depth, depth), f32),
@@ -402,8 +441,8 @@
             pltpu.VMEM(piece, f32),
             pltpu.VMEM(piece, f32),
             pltpu.VMEM(piece, f32),
-            dma((5, 3)),
-            dma((5, 3)),
+            dma((5, pieces)),
+            dma((5, pieces)),
             dma((4,)),
             dma((4,)),
             dma((2, count)),
@@ -414,12 +453,17 @@
             dma((count,)),
             dma((count,)),
             dma((count,)),
+            pltpu.VMEM(edges.shape, f32),
+            pltpu.VMEM(edges.shape, f32),
+            pltpu.VMEM(edges.shape, f32),
+            pltpu.VMEM(nodes.shape, f32),
+            dma((5,)),
         ],
         compiler_params=pltpu.CompilerParams(
             collective_id=0, has_side_effects=True, vmem_limit_bytes=56 * 1024 * 1024
         ),
     )(
-        nodes, edges, senders[None, :], receivers[None, :], halo, drop_mask[None, :], w_in, w_out, cotangent
+        nodes, edges, senders, receivers, halo_rows, drop_mask, w_in, w_out, cotangent
     )
 
 

time: 86.3 us -> 79.3 us (0.919)
  Pallas kernels: 76.4 us -> 72.9 us
  local copies, waits for them, and re-layouts: 8.89 us -> 5.47 us
    pallas_call x1, Pallas kernels: 76.4 us -> 72.9 us  [body(): pl.pallas_call(functools.partial(kernel, sizes), out_shape=(jax.ShapeDtyp...]
    broadcast_in_dim x4 -> x0, local copies, waits for them, and re-layouts: 1.69 us -> none  [the longest x1 0.56 us: body(): senders[None, :]]
    unnamed x14 -> x8, local copies, waits for them, and re-layouts: 5.8 us -> 5.47 us
where the time goes in v2:
time: 79.3 us; the launch traced here: 79 us
  Pallas kernels  72.9 us (92%)
  local copies, waits for them, and re-layouts  5.47 us (7%)
    pallas_call x1, Pallas kernels, body(): pl.pallas_call(functools.partial(kernel, sizes), out_shape=(jax.ShapeDtyp...  72.9 us
    unnamed x8, local copies, waits for them, and re-layouts  5.47 us

profile of v2, /device:TPU:0, one launch (start us, length us, event | category | flops | bytes accessed | tf_op | source)
XLA Modules:
  0.0 79.0 jit_solution(16081876130675829115)
XLA Ops:
  0.6 72.9 %shard_map.120 = (f32[48,512]{1,0:T(8,128)}, f32[384,512]{1,0:T(8,128)}, f32[384,512]{1,0:T(8,128)}, f32[128,512]{1,0:T(8,128)}) custom-call(f32[48,512]{1,0:T(8,128)} %nodes_ref.1, f32[384,512]{1,0:T(8,128)} %edges_ref.1, s32[384]{0:T(512)} %senders_ref.1, s32[384]{0:T(512)} %receivers_ref.1, s32[24]{0:T(128)} %halo_ref.1, s32[384]{0:T(512)} %drop_ref.1, ...), custom_call_target="tpu_custom_call" | custom-call | tf_op jit(solution)/shard_map/pallas_call | solution.py:418
  73.5 1.5 %copy.17 = f32[48,512]{1,0:T(8,128)} copy(f32[48,512]{1,0:T(8,128)} %get-tuple-element.8) | data formatting | bytes 196608
  75.1 0.0 copy-start
  75.1 2.1 %copy.18 = f32[384,512]{1,0:T(8,128)} copy(f32[384,512]{1,0:T(8,128)} %get-tuple-element.9) | data formatting | bytes 1572864
  77.2 0.0 copy-done
  77.2 0.0 copy-start.1
  77.2 0.9 %copy.19 = f32[384,512]{1,0:T(8,128)} copy(f32[384,512]{1,0:T(8,128)S(1)} %copy-done) | data formatting | bytes 1572864
  78.1 0.2 copy-done.1
  78.3 0.7 copy.20
Async XLA Ops:
  75.1 2.1 %copy-start = (f32[384,512]{1,0:T(8,128)S(1)}, f32[384,512]{1,0:T(8,128)}, u32[]{:S(2)}) copy-start(f32[384,512]{1,0:T(8,128)} %get-tuple-element.10) | copy-start | bytes 2359300
  77.2 1.1 %copy-start.1 = (f32[128,512]{1,0:T(8,128)S(1)}, f32[128,512]{1,0:T(8,128)}, u32[]{:S(2)}) copy-start(f32[128,512]{1,0:T(8,128)} %get-tuple-element.11) | copy-start | bytes 786436

commit v3 on v2

--- a/solution.py
+++ b/solution.py
@@ -359,19 +359,26 @@
         result = gwout_ref if kind == 1 else gwin_ref
         result[pl.ds(start, span.size)] = total[blocks[number][2]] * factor
 
-    lag = 2
-    for number in range(len(blocks) + lag):
-        if number < len(blocks):
-            collect(number)
-        if number == 4:
+    ends_at = [span.start + span.size for _, _, span in blocks]
+    done = 0
+    for number in range(len(blocks)):
+        collect(number)
+        if number == first_in:
             back_prev.wait_recv()
             back_next.wait_recv()
             gnodes_ref[...] = own[...] + product2(halo_hot, split(back_recv[...]), (1, 0))
-        if number >= lag:
-
-            @pl.when(has_outer)
-            def _():
-                finish(number - lag, True)
+        ready = done
+        while ready < len(blocks) and ends_at[number] - ends_at[ready] >= sizes["lag"]:
+            ready += 1
+        if number == len(blocks) - 1:
+            ready = len(blocks)
+
+        @pl.when(has_outer)
+        def _():
+            for earlier in range(done, ready):
+                finish(earlier, True)
+
+        done = ready
 
     @pl.when(jnp.logical_not(has_outer))
     def _():
@@ -391,6 +398,34 @@
     def _():
         for number in range(len(blocks)):
             outward(number).wait_send()
+
+
+emit_pieces = 4
+
+
+def emit(*refs):
+    copies = []
+    for number in range(4):
+        source, target = refs[number], refs[4 + number]
+        size = source.shape[0] // emit_pieces
+        if size % 8:
+            spans = [pl.ds(0, source.shape[0])]
+        else:
+            spans = [pl.ds(start, size) for start in range(0, source.shape[0], size)]
+        for place, span in enumerate(spans):
+            copies.append(
+                (
+                    pltpu.make_async_copy(source.at[span], refs[8 + number].at[span], refs[12].at[number, place]),
+                    pltpu.make_async_copy(refs[8 + number].at[span], target.at[span], refs[13].at[number, place]),
+                )
+            )
+    for load, _ in copies:
+        load.start()
+    for load, store in copies:
+        load.wait()
+        store.start()
+    for _, store in copies:
+        store.wait()
 
 
 def body(mesh_shape, nodes, edges, senders, receivers, halo_rows, drop_mask, w_in, w_out, cotangent):
@@ -404,8 +439,9 @@
         "dom": doms,
         "gather_in": (3, 3, 3, 2, 1),
         "gather_out": (1, 1),
-        "sum_out": (1, 1, 2, 4),
-        "sum_in": (8, 8, 8, 8, 4, 4, 2, 2, 2, 1, 1),
+        "lag": 64,
+        "sum_out": (1, 1, 1, 1),
+        "sum_in": (4, 4, 4, 4, 4, 4, 4, 4, 4, 4, 2, 2, 2, 1, 1),
         "halo": halo_size,
         "factor": 1.0 / math.sqrt(count_edges * doms * mesh_shape["mp"]),
     }
@@ -415,7 +451,7 @@
     piece = (w_in.shape[0] + w_out.shape[0], depth)
     hbm = pl.BlockSpec(memory_space=pl.ANY)
     dma = pltpu.SemaphoreType.DMA
-    return pl.pallas_call(
+    results = pl.pallas_call(
         functools.partial(kernel, sizes),
         out_shape=(
             jax.ShapeDtypeStruct(nodes.shape, f32),
@@ -465,6 +501,13 @@
     )(
         nodes, edges, senders, receivers, halo_rows, drop_mask, w_in, w_out, cotangent
     )
+    return pl.pallas_call(
+        emit,
+        out_shape=tuple(jax.ShapeDtypeStruct(result.shape, f32) for result in results),
+        in_specs=[hbm] * 4,
+        out_specs=(hbm,) * 4,
+        scratch_shapes=[pltpu.VMEM(result.shape, f32) for result in results] + [dma((4, emit_pieces))] * 2,
+    )(*results)
 
 
 def solution(mesh):

time: 79.3 us -> 73.6 us (0.928)
  local copies, waits for them, and re-layouts: 5.47 us -> 0 us
    unnamed x8 -> x0, local copies, waits for them, and re-layouts: 5.47 us -> none
    pallas_call x1, Pallas kernels: 72.9 us -> 70.2 us  [body(): pl.pallas_call(functools.partial(kernel, sizes), out_shape=(jax.ShapeDtyp...]
    pallas_call x0 -> x1, Pallas kernels: none -> 2.56 us  [body(): pl.pallas_call(emit, out_shape=tuple((jax.ShapeDtypeStruct(result.shape,...]
where the time goes in v3:
time: 73.6 us; the launch traced here: 73.4 us
  Pallas kernels  72.8 us (99%)
    pallas_call x1, Pallas kernels, body(): pl.pallas_call(functools.partial(kernel, sizes), out_shape=(jax.ShapeDtyp...  70.2 us
    pallas_call x1, Pallas kernels, body(): pl.pallas_call(emit, out_shape=tuple((jax.ShapeDtypeStruct(result.shape,...  2.56 us

profile of v3, /device:TPU:0, one launch (start us, length us, event | category | flops | bytes accessed | tf_op | source)
XLA Modules:
  0.0 73.4 jit_solution(7055167311776930776)
XLA Ops:
  0.6 70.2 %shard_map.120 = (f32[48,512]{1,0:T(8,128)}, f32[384,512]{1,0:T(8,128)}, f32[384,512]{1,0:T(8,128)}, f32[128,512]{1,0:T(8,128)}) custom-call(f32[48,512]{1,0:T(8,128)} %nodes_ref.1, f32[384,512]{1,0:T(8,128)} %edges_ref.1, s32[384]{0:T(512)} %senders_ref.1, s32[384]{0:T(512)} %receivers_ref.1, s32[24]{0:T(128)} %halo_ref.1, s32[384]{0:T(512)} %drop_ref.1, ...), custom_call_target="tpu_custom_call" | custom-call | tf_op jit(solution)/shard_map/pallas_call | solution.py:454
  70.9 2.6 %shard_map.121 = (f32[48,512]{1,0:T(8,128)}, f32[384,512]{1,0:T(8,128)}, f32[384,512]{1,0:T(8,128)}, f32[128,512]{1,0:T(8,128)}) custom-call(f32[48,512]{1,0:T(8,128)} %get-tuple-element.8.refs_0_, f32[384,512]{1,0:T(8,128)} %get-tuple-element.9.refs_1_, f32[384,512]{1,0:T(8,128)} %get-tuple-element.10.refs_2_, f32[128,512]{1,0:T(8,128)} %get-tuple-element.11.refs_3_), custom_call_target="tpu_custom_call" | custom-call | tf_op jit(solution)/shard_map/pallas_call | solution.py:504

commit v4 on v3

--- a/solution.py
+++ b/solution.py
@@ -160,22 +160,6 @@
     table[0:count_nodes] = nodes
     table[slots : slots + count_nodes] = nodes
 
-    senders = senders_ref[...].reshape(1, count_edges)
-    senders = jnp.where(senders < count_nodes + halo_size, senders, senders + (padded - halo_size))
-    receivers = receivers_ref[...].reshape(1, count_edges)
-    targets = slots + jnp.minimum(receivers, count_nodes - 1)
-    total_slots = slots + count_nodes
-    index = lax.broadcasted_iota(jnp.int32, (total_slots, count_edges), 0)
-    hot = jnp.where((index == senders) | (index == targets), 1.0, 0.0)
-    hot_t = hot.astype(bf16)
-    hot = jnp.transpose(hot).astype(bf16)
-    keep = jnp.where((receivers < count_nodes) & (drop_ref[...].reshape(1, count_edges) == 1), f32(keep_scale), f32(0.0))
-    keep = jnp.transpose(jnp.broadcast_to(keep, (128, count_edges)))[:, :1]
-
-    for load in loads:
-        load.wait()
-    edges = split(edges_in[...])
-
     peer_x, peer_core, peer_far = 2 * far + c, 2 * x + (1 - c), 2 * far + (1 - c)
 
     def forward_x(number):
@@ -198,11 +182,30 @@
             fy_copies.append(copy)
 
     ahead = 2
-    for number in range(count_in + ahead):
+    forward_x(0)
+    senders = senders_ref[...].reshape(1, count_edges)
+    senders = jnp.where(senders < count_nodes + halo_size, senders, senders + (padded - halo_size))
+    receivers = receivers_ref[...].reshape(1, count_edges)
+    targets = slots + jnp.minimum(receivers, count_nodes - 1)
+    total_slots = slots + count_nodes
+    index = lax.broadcasted_iota(jnp.int32, (total_slots, count_edges), 0)
+    hot = jnp.where((index == senders) | (index == targets), 1.0, 0.0)
+    hot_t = hot.astype(bf16)
+    hot = jnp.transpose(hot).astype(bf16)
+    forward_x(1)
+    keep = jnp.where((receivers < count_nodes) & (drop_ref[...].reshape(1, count_edges) == 1), f32(keep_scale), f32(0.0))
+    keep = jnp.transpose(jnp.broadcast_to(keep, (128, count_edges)))[:, :1]
+
+    forward_x(2)
+    forward_y(0)
+    for load in loads:
+        load.wait()
+    edges = split(edges_in[...])
+
+    for number in range(ahead + 1, count_in + ahead):
         if number < last:
             forward_x(number)
-        if number >= ahead:
-            forward_y(number - ahead)
+        forward_y(number - ahead)
     whole_in.wait_recv()
     to_next.wait_recv()
     to_prev.wait_recv()
@@ -290,6 +293,57 @@
             copy.start()
             x_grad_copies[number] = copy
 
+    def inward(number, to_mid):
+        landing = (from_inner, inner_rsem) if to_mid else (from_outer, outer_rsem)
+        return remote(acc.at[blocks[number][2]], landing[0].at[blocks[number][2]], inward_ssem.at[number], landing[1].at[number], inner_peer)
+
+    def outward(number):
+        return remote(total.at[blocks[number][2]], from_inner.at[blocks[number][2]], outward_ssem.at[number], inner_rsem.at[number], outer_peer)
+
+    def gather(number):
+        core_copies[1, number].wait_recv()
+        x_grad_copies[number].wait_recv()
+        acc[blocks[number][2]] = grad_rows(m, number)[...] + from_core[1, blocks[number][2]] + from_x[blocks[number][2]]
+
+        @pl.when(jnp.logical_not(has_outer))
+        def _():
+            pass_inward(number)
+
+    def pass_inward(number):
+        @pl.when(is_mid)
+        def _():
+            inward(number, True).start()
+
+        @pl.when(jnp.logical_not(is_mid))
+        def _():
+            inward(number, False).start()
+
+    def collect(number):
+        @pl.when(has_outer)
+        def _():
+            inward(number, False).wait_recv()
+            acc[blocks[number][2]] = acc[blocks[number][2]] + from_outer[blocks[number][2]]
+            pass_inward(number)
+
+    factor = f32(sizes["factor"])
+
+    def finish(number, sends):
+        kind, start, span = blocks[number]
+        inward(number, True).wait_recv()
+
+        @pl.when(is_mid)
+        def _():
+            total[blocks[number][2]] = acc[blocks[number][2]] + from_inner[blocks[number][2]]
+
+        @pl.when(jnp.logical_not(is_mid))
+        def _():
+            total[blocks[number][2]] = from_inner[blocks[number][2]]
+
+        if sends:
+            outward(number).start()
+        result = gwout_ref if kind == 1 else gwin_ref
+        result[pl.ds(start, span.size)] = total[blocks[number][2]] * factor
+
     early, late = range(first_in), range(first_in, len(blocks))
     swap_cores(early)
     grad_hidden = split(product3(grad_message, w_o, (1, 1)) * slope)
@@ -300,6 +354,9 @@
     gin[2 * depth : 3 * depth] = product3(table_pair, split(jnp.where(slot < slots, 0.0, sums)), (0, 0))
     gin[0:depth] = product3(edges, grad_hidden, (0, 0))
     swap_cores(late)
+    begun = 2
+    for number in range(begun):
+        gather(number)
 
     sums = split(sums)
     grad_table = product3(pick(sums, slice(0, slots)), w_b, (1, 1))
@@ -315,53 +372,11 @@
     edges_out = pltpu.make_async_copy(grad_edges, gedges_ref, local_sem.at[4])
     edges_out.start()
 
-    def inward(number, to_mid):
-        landing = (from_inner, inner_rsem) if to_mid else (from_outer, outer_rsem)
-        return remote(acc.at[blocks[number][2]], landing[0].at[blocks[number][2]], inward_ssem.at[number], landing[1].at[number], inner_peer)
-
-    def outward(number):
-        return remote(total.at[blocks[number][2]], from_inner.at[blocks[number][2]], outward_ssem.at[number], inner_rsem.at[number], outer_peer)
-
-    def collect(number):
-        core_copies[1, number].wait_recv()
-        x_grad_copies[number].wait_recv()
-        acc[blocks[number][2]] = grad_rows(m, number)[...] + from_core[1, blocks[number][2]] + from_x[blocks[number][2]]
-
-        @pl.when(has_outer)
-        def _():
-            inward(number, False).wait_recv()
-            acc[blocks[number][2]] = acc[blocks[number][2]] + from_outer[blocks[number][2]]
-
-        @pl.when(is_mid)
-        def _():
-            inward(number, True).start()
-
-        @pl.when(jnp.logical_not(is_mid))
-        def _():
-            inward(number, False).start()
-
-    factor = f32(sizes["factor"])
-
-    def finish(number, sends):
-        kind, start, span = blocks[number]
-        inward(number, True).wait_recv()
-
-        @pl.when(is_mid)
-        def _():
-            total[blocks[number][2]] = acc[blocks[number][2]] + from_inner[blocks[number][2]]
-
-        @pl.when(jnp.logical_not(is_mid))
-        def _():
-            total[blocks[number][2]] = from_inner[blocks[number][2]]
-
-        if sends:
-            outward(number).start()
-        result = gwout_ref if kind == 1 else gwin_ref
-        result[pl.ds(start, span.size)] = total[blocks[number][2]] * factor
-
     ends_at = [span.start + span.size for _, _, span in blocks]
     done = 0
     for number in range(len(blocks)):
+        if number >= begun:
+            gather(number)
         collect(number)
         if number == first_in:
             back_prev.wait_recv()

time: 73.6 us -> 72.1 us (0.980)
  Pallas kernels: 72.8 us -> 71.3 us
    pallas_call x1, Pallas kernels: 70.2 us -> 68.7 us  [body(): pl.pallas_call(functools.partial(kernel, sizes), out_shape=(jax.ShapeDtyp...]
where the time goes in v4:
time: 72.1 us; the launch traced here: 71.9 us
  Pallas kernels  71.3 us (99%)
    pallas_call x1, Pallas kernels, body(): pl.pallas_call(functools.partial(kernel, sizes), out_shape=(jax.ShapeDtyp...  68.7 us
    pallas_call x1, Pallas kernels, body(): pl.pallas_call(emit, out_shape=tuple((jax.ShapeDtypeStruct(result.shape,...  2.56 us

profile of v4, /device:TPU:0, one launch (start us, length us, event | category | flops | bytes accessed | tf_op | source)
XLA Modules:
  0.0 71.9 jit_solution(7894279060820897119)
XLA Ops:
  0.6 68.7 %shard_map.120 = (f32[48,512]{1,0:T(8,128)}, f32[384,512]{1,0:T(8,128)}, f32[384,512]{1,0:T(8,128)}, f32[128,512]{1,0:T(8,128)}) custom-call(f32[48,512]{1,0:T(8,128)} %nodes_ref.1, f32[384,512]{1,0:T(8,128)} %edges_ref.1, s32[384]{0:T(512)} %senders_ref.1, s32[384]{0:T(512)} %receivers_ref.1, s32[24]{0:T(128)} %halo_ref.1, s32[384]{0:T(512)} %drop_ref.1, ...), custom_call_target="tpu_custom_call" | custom-call | tf_op jit(solution)/shard_map/pallas_call | solution.py:469
  69.4 2.6 %shard_map.121 = (f32[48,512]{1,0:T(8,128)}, f32[384,512]{1,0:T(8,128)}, f32[384,512]{1,0:T(8,128)}, f32[128,512]{1,0:T(8,128)}) custom-call(f32[48,512]{1,0:T(8,128)} %get-tuple-element.8.refs_0_, f32[384,512]{1,0:T(8,128)} %get-tuple-element.9.refs_1_, f32[384,512]{1,0:T(8,128)} %get-tuple-element.10.refs_2_, f32[128,512]{1,0:T(8,128)} %get-tuple-element.11.refs_3_), custom_call_target="tpu_custom_call" | custom-call | tf_op jit(solution)/shard_map/pallas_call | solution.py:519
